TPU v7x, 256 devices: a whole 4x4x8 slice. The times are simulated.
256 devices in a mesh: dp: 16 (over x, y_hi, core), vocab: 8 (over z), tensor: 2 (over y_lo).
Axes of the slice: x: 4, y: 4 (y_hi: 2, y_lo: 2; y = y_hi * 2 + y_lo), z: 8, core: 2. Of those that a mesh axis runs over, the one named last changes fastest.
Arguments:
- residual: bfloat16 [1408, 4096], P('dp', 'tensor'), may hold values from -400 to 400
- norm_gain: float32 [4096], P('tensor'), may hold values from 0.1 to 1.9
- gain_dir: float32 [4096], P('tensor'), may hold values from -6 to 6
- head_weight: bfloat16 [4096, 81920], P('tensor', ('dp', 'vocab')), may hold values from -0.8 to 0.8
- head_dir: bfloat16 [4096, 81920], P('tensor', ('dp', 'vocab')), may hold values from -0.25 to 0.25
- sampled: int32 [1408], replicated, may hold values from 0 to 81919
Outputs:
- fisher_head: float32 [4096, 81920], P('tensor', ('dp', 'vocab'))
- fisher_gain: float32 [4096], P('tensor')
All inputs are finite; a program needn't handle non-finite values.
Results may differ from a plain program's by a relative error of at most 0.012.
The roundings to bfloat16 on the way count: a program that leaves them out, or rounds other values in their place, can miss the bound.
Values may be sent and summed in bfloat16 or wider, within the bound.
No kernel may reach another device: no remote copies, remote signals or barrier semaphores. Data moves between devices by JAX's collectives and lax.ppermute only.
A program may use at most 128 MiB of HBM per device.

v0:
```python
import jax
import jax.numpy as jnp
from jax import lax
from jax.sharding import PartitionSpec as P

EPSILON = 1e-06


def local(residual, norm_gain, gain_dir, head_weight, head_dir, sampled):
    full_width = residual.shape[1] * lax.axis_size("tensor")
    entries = residual.astype(jnp.float32)
    squares = lax.psum(jnp.sum(entries * entries, axis=1), "tensor")
    normed = (entries * lax.rsqrt(squares / full_width + EPSILON)[:, None]).astype(jnp.bfloat16)
    gathered = lax.all_gather(normed, "dp", axis=0, tiled=True)
    spread = gathered.astype(jnp.float32)
    hidden = (spread * norm_gain).astype(jnp.bfloat16)
    tangent = (spread * gain_dir).astype(jnp.bfloat16)
    logits = jnp.dot(hidden, head_weight, preferred_element_type=jnp.float32)
    tangent_logits = jnp.dot(hidden, head_dir, preferred_element_type=jnp.float32) + jnp.dot(
        tangent, head_weight, preferred_element_type=jnp.float32
    )
    logits, tangent_logits = (
        lax.psum_scatter(logits, "tensor", scatter_dimension=0, tiled=True),
        lax.psum_scatter(tangent_logits, "tensor", scatter_dimension=0, tiled=True),
    )
    share_rows = logits.shape[0]
    picked_ids = lax.dynamic_slice_in_dim(
        sampled, lax.axis_index("tensor") * share_rows, share_rows
    )
    vocab_dev = head_weight.shape[1]
    offset = (lax.axis_index("dp") * lax.axis_size("vocab") + lax.axis_index("vocab")) * vocab_dev
    is_picked = lax.broadcasted_iota(jnp.int32, logits.shape, 1) == (picked_ids - offset)[:, None]
    picked_part = jnp.sum(jnp.where(is_picked, tangent_logits, 0.0), axis=1)
    row_top = lax.pmax(jnp.max(logits, axis=1), ("dp", "vocab"))
    scaled_exp = jnp.exp(logits - row_top[:, None])
    row_total, weighted, picked = lax.psum(
        (jnp.sum(scaled_exp, axis=1), jnp.sum(scaled_exp * tangent_logits, axis=1), picked_part),
        ("dp", "vocab"),
    )
    row_probs = scaled_exp / row_total[:, None]
    row_score = picked - weighted / row_total
    cotangent = (row_score[:, None] * (is_picked.astype(jnp.float32) - row_probs)).astype(
        jnp.bfloat16
    )
    full_cot = lax.all_gather(cotangent, "tensor", axis=0, tiled=True)
    product = lax.dot_general(
        gathered, full_cot, (((0,), (0,)), ((), ())), preferred_element_type=jnp.float32
    )
    fisher_head = norm_gain[:, None] * product
    fisher_gain = lax.psum(
        jnp.sum(head_weight.astype(jnp.float32) * product, axis=1), ("dp", "vocab")
    )
    return (fisher_head, fisher_gain)


def solution(mesh):
    in_specs = (
        P("dp", "tensor"),
        P("tensor"),
        P("tensor"),
        P("tensor", ("dp", "vocab")),
        P("tensor", ("dp", "vocab")),
        P(),
    )
    out_specs = (P("tensor", ("dp", "vocab")), P("tensor"))
    return jax.shard_map(local, mesh=mesh, in_specs=in_specs, out_specs=out_specs, check_vma=False)
```

profile of v0, /device:TPU:8, one launch (start us, length us, event | category | flops | bytes accessed | tf_op | source)
XLA Modules:
  0.0 1515.0 jit_solution(15969742382134527424)
XLA Ops:
  7.2 0.0 copy-start
  7.2 0.0 all-gather.3.cloned.1.call-start
  7.2 1.3 fusion.13
  8.5 5.1 psum.35
  13.6 1.9 fusion.14
  15.5 0.0 all-gather.3.cloned.1.call-update
  15.5 0.0 reduce-scatter.5.cloned.1.call-start
  15.6 69.0 %all-gather.3.cloned.1.call-done = bf16[1408,2048]{1,0:T(8,128)(2,1)} async-done(((bf16[88,2048]{1,0:T(8,128)(2,1)}), bf16[1408,2048]{1,0:T(8,128)(2,1)}) %all-gather.3.cloned.1.call-update) | async-done | bytes 5767184 | tf_op jit(solution)/shard_map/all_gather | solution.py:14
  84.6 9.9 fusion.5
  94.5 0.0 reduce-scatter.5.cloned.1.call-update
  94.5 0.0 copy-start.3
  94.6 0.0 reduce-scatter.3.cloned.1.call-start
  94.6 0.6 copy-done.2
  95.2 7.4 fusion.2
  102.7 9.2 fusion.9
  111.9 0.0 reduce-scatter.3.cloned.1.call-update
  111.9 0.0 all-gather.5.cloned.1.call-start
  112.0 0.6 copy-done.1
  112.6 0.1 dynamic-slice_subtract_fusion
  112.7 34.0 %reduce-scatter.5.cloned.1.call-done = f32[704,640]{1,0:T(8,128)} async-done(((f32[1408,640]{1,0:T(8,128)}), f32[704,640]{1,0:T(8,128)}) %reduce-scatter.5.cloned.1.call-update) | async-done | bytes 1802256 | tf_op jit(solution)/shard_map/reduce_scatter | solution.py:23
  146.7 1.7 reduce_max.9
  148.3 331.6 %pmax.7 = f32[704]{0:T(1024)S(1)} all-reduce(f32[704]{0:T(1024)S(1)} %reduce_max.9), channel_id=1, replica_groups=mesh['dp'=16,'vocab'=8,'tensor'=2] {'dp','vocab'}, use_global_device_ids=true, to_apply=%region_7.8 | all-reduce | flops 704 | bytes 5632 | tf_op jit(solution)/shard_map/pmax | solution.py:34
  480.0 0.0 reduce-scatter.3.cloned.1.call-done
  480.0 2.9 multiply_reduce_fusion.1
  482.9 644.7 %all-reduce = (f32[704]{0:T(1024)S(1)}, f32[704]{0:T(1024)S(1)}, f32[704]{0:T(1024)S(1)}) all-reduce(f32[704]{0:T(1024)S(1)} %get-tuple-element.5, f32[704]{0:T(1024)S(1)} %get-tuple-element.6, f32[704]{0:T(1024)S(1)} %get-tuple-element.4), channel_id=1, replica_groups=mesh['dp'=16,'vocab'=8,'tensor'=2] {'dp','vocab'}, use_global_device_ids=true, to_apply=%region_11.12 | all-reduce | flops 2112 | bytes 16896 | tf_op jit(solution)/shard_map/psum | solution.py:36
  1127.6 2.7 multiply_convert_fusion
  1130.4 0.0 all-gather.5.cloned.1.call-update
  1130.4 4.4 copy.8
  1134.8 21.6 %all-gather.5.cloned.1.call-done = bf16[1408,640]{1,0:T(8,128)(2,1)} async-done(((bf16[704,640]{1,0:T(8,128)(2,1)}), bf16[1408,640]{1,0:T(8,128)(2,1)}) %all-gather.5.cloned.1.call-update) | async-done | bytes 1802256 | tf_op jit(solution)/shard_map/all_gather | solution.py:45
  1156.4 10.9 multiply_reduce_fusion
  1167.3 5.9 copy.9
  1173.2 335.3 %psum.39 = f32[2048]{0:T(1024)} all-reduce(f32[2048]{0:T(1024)S(1)} %get-tuple-element.10), channel_id=1, replica_groups=mesh['dp'=16,'vocab'=8,'tensor'=2] {'dp','vocab'}, use_global_device_ids=true, to_apply=%region_13.14 | all-reduce | flops 2048 | bytes 16384 | tf_op jit(solution)/shard_map/psum | solution.py:50
  (6 shorter events, 0.0 us)
Async XLA Ops:
  7.2 95.5 %copy-start = (bf16[2048,640]{1,0:T(8,128)(2,1)S(1)}, bf16[2048,640]{1,0:T(8,128)(2,1)}, u32[]{:S(2)}) copy-start(bf16[2048,640]{1,0:T(8,128)(2,1)} %param.10) | copy-start | bytes 7864324
  7.2 77.4 %all-gather.3.cloned.1.call-start = ((), (), s32[]{:S(2)}) async-start(), calls=%async_computation.2 | async-start | bytes 6127616 | tf_op jit(solution)/shard_map/all_gather | solution.py:14
  15.5 131.2 %reduce-scatter.5.cloned.1.call-start = ((), (), s32[]{:S(2)}) async-start(), calls=%async_computation.4 | async-start | bytes 5406720 | tf_op jit(solution)/shard_map/reduce_scatter | solution.py:23
  94.5 0.7 copy-start.2
  94.5 8.1 copy-start.3
  94.6 385.4 %reduce-scatter.3.cloned.1.call-start = ((), (), s32[]{:S(2)}) async-start(), calls=%async_computation.3 | async-start | bytes 5406720 | tf_op jit(solution)/shard_map/reduce_scatter | solution.py:24
  111.9 0.7 copy-start.1
  111.9 1044.5 %all-gather.5.cloned.1.call-start = ((), (), s32[]{:S(2)}) async-start(), calls=%async_computation.5 | async-start | bytes 2703360 | tf_op jit(solution)/shard_map/all_gather | solution.py:45
Sparse Core Ops, SparseCore 0:
  15.6 68.9 all-gather.2
  94.7 51.9 reduce-scatter.4
  149.3 54.8 reduce-scatter.2
  1130.5 25.8 all-gather.4
where the time goes:
time: 1520 us
  blocking collectives  1320 us (87%)
  waiting for transfers between devices  125 us (8%)
  matrix products  37.5 us (2%)
    psum x1, blocking collectives, local(): lax.psum((jnp.sum(scaled_exp, axis=1), jnp.sum(scaled_exp * tangent_logit...  645 us
    psum x1, blocking collectives, local(): lax.psum(jnp.sum(head_weight.astype(jnp.float32) * product, axis=1), ('dp...  335 us
    pmax x1, blocking collectives, local(): row_top = lax.pmax(jnp.max(logits, axis=1), ('dp', 'vocab'))  332 us
    all_gather x1, waiting for transfers between devices, local(): gathered = lax.all_gather(normed, 'dp', axis=0, tiled=True)  69 us
    reduce_scatter x1, waiting for transfers between devices, local(): lax.psum_scatter(logits, 'tensor', scatter_dimension=0, tiled=True)  34 us
  transfers between devices with their start and end apart: 4, of which 3 were waited for; matrix products, arithmetic and copies ran while one was open for 2% of the time, Pallas kernels for 0%

commit v1 on v0

--- a/solution.py
+++ b/solution.py
@@ -47,9 +47,9 @@
         gathered, full_cot, (((0,), (0,)), ((), ())), preferred_element_type=jnp.float32
     )
     fisher_head = norm_gain[:, None] * product
-    fisher_gain = lax.psum(
-        jnp.sum(head_weight.astype(jnp.float32) * product, axis=1), ("dp", "vocab")
-    )
+    part = jnp.sum(head_weight.astype(jnp.float32) * product, axis=1)
+    pieces = lax.all_gather(part, ("dp", "vocab"), axis=0, tiled=False)
+    fisher_gain = pieces.sum(axis=0)
     return (fisher_head, fisher_gain)
 
 

time: 1520 us -> 1290 us (0.85)
  blocking collectives: 1320 us -> 981 us
  waiting for transfers between devices: 125 us -> 223 us
    psum x1 -> x0, blocking collectives: 335 us -> none  [local(): lax.psum(jnp.sum(head_weight.astype(jnp.float32) * product, axis=1), ('dp...]
    all_gather x0 -> x1, waiting for transfers between devices: none -> 98.7 us  [local(): pieces = lax.all_gather(part, ('dp', 'vocab'), axis=0, tiled=False)]
  transfers between devices with their start and end apart: 4 -> 5, of which waited for: 3 -> 4; matrix products, arithmetic and copies ran while one was open for 2% -> 2% of each run, Pallas kernels for 0% -> 0%
where the time goes in v1:
time: 1290 us; the launch traced here: 1280 us
  blocking collectives  981 us (76%)
  waiting for transfers between devices  223 us (17%)
  matrix products  38 us (3%)
  local copies, waits for them, and re-layouts  13.9 us (1%)
  between operations  13.9 us (1%)
    psum x1, blocking collectives, local(): lax.psum((jnp.sum(scaled_exp, axis=1), jnp.sum(scaled_exp * tangent_logit...  645 us
    pmax x1, blocking collectives, local(): row_top = lax.pmax(jnp.max(logits, axis=1), ('dp', 'vocab'))  332 us
    all_gather x1, waiting for transfers between devices, local(): pieces = lax.all_gather(part, ('dp', 'vocab'), axis=0, tiled=False)  98.7 us
    all_gather x1, waiting for transfers between devices, local(): gathered = lax.all_gather(normed, 'dp', axis=0, tiled=True)  69 us
    reduce_scatter x1, waiting for transfers between devices, local(): lax.psum_scatter(logits, 'tensor', scatter_dimension=0, tiled=True)  34 us
  transfers between devices with their start and end apart: 5, of which 4 were waited for; matrix products, arithmetic and copies ran while one was open for 2% of the time, Pallas kernels for 0%

profile of v1, /device:TPU:8, one launch (start us, length us, event | category | flops | bytes accessed | tf_op | source)
XLA Modules:
  0.0 1283.3 jit_solution(13389705201986357541)
XLA Ops:
  7.2 0.0 all-gather.5.cloned.1.call-start
  7.2 1.3 fusion.13
  8.5 5.1 psum.28
  13.6 1.9 fusion.14
  15.5 0.0 reduce-scatter.5.cloned.1.call-start
  15.6 69.0 %all-gather.5.cloned.1.call-done = bf16[1408,2048]{1,0:T(8,128)(2,1)} async-done(((bf16[88,2048]{1,0:T(8,128)(2,1)}), bf16[1408,2048]{1,0:T(8,128)(2,1)}) %all-gather.5.cloned.1.call-update) | async-done | bytes 5767184 | tf_op jit(solution)/shard_map/all_gather | solution.py:14
  84.6 9.9 fusion.5
  94.6 0.0 reduce-scatter.3.cloned.1.call-start
  94.6 0.6 copy-done.2
  95.2 7.4 fusion.2
  102.7 9.2 fusion.9
  111.9 0.0 reduce-scatter.3.cloned.1.call-update
  111.9 0.0 all-gather.7.cloned.1.call-start
  112.0 0.6 copy-done.1
  112.6 0.1 dynamic-slice_subtract_fusion
  112.7 34.0 %reduce-scatter.5.cloned.1.call-done = f32[704,640]{1,0:T(8,128)} async-done(((f32[1408,640]{1,0:T(8,128)}), f32[704,640]{1,0:T(8,128)}) %reduce-scatter.5.cloned.1.call-update) | async-done | bytes 1802256 | tf_op jit(solution)/shard_map/reduce_scatter | solution.py:23
  146.7 1.7 reduce_max.9
  148.3 331.6 %pmax.7 = f32[704]{0:T(1024)S(1)} all-reduce(f32[704]{0:T(1024)S(1)} %reduce_max.9), channel_id=1, replica_groups=mesh['dp'=16,'vocab'=8,'tensor'=2] {'dp','vocab'}, use_global_device_ids=true, to_apply=%region_7.8 | all-reduce | flops 704 | bytes 5632 | tf_op jit(solution)/shard_map/pmax | solution.py:34
  480.0 0.0 reduce-scatter.3.cloned.1.call-done
  480.0 2.9 multiply_reduce_fusion.1
  482.9 644.7 %all-reduce = (f32[704]{0:T(1024)S(1)}, f32[704]{0:T(1024)S(1)}, f32[704]{0:T(1024)S(1)}) all-reduce(f32[704]{0:T(1024)S(1)} %get-tuple-element.9, f32[704]{0:T(1024)S(1)} %get-tuple-element.10, f32[704]{0:T(1024)S(1)} %get-tuple-element.8), channel_id=1, replica_groups=mesh['dp'=16,'vocab'=8,'tensor'=2] {'dp','vocab'}, use_global_device_ids=true, to_apply=%region_11.12 | all-reduce | flops 2112 | bytes 16896 | tf_op jit(solution)/shard_map/psum | solution.py:36
  1127.6 2.7 multiply_convert_fusion
  1130.4 0.0 all-gather.7.cloned.1.call-update
  1130.4 0.0 all-gather.9.cloned.1.call-start
  1130.4 4.4 copy.12
  1134.8 21.6 %all-gather.7.cloned.1.call-done = bf16[1408,640]{1,0:T(8,128)(2,1)} async-done(((bf16[704,640]{1,0:T(8,128)(2,1)}), bf16[1408,640]{1,0:T(8,128)(2,1)}) %all-gather.7.cloned.1.call-update) | async-done | bytes 1802256 | tf_op jit(solution)/shard_map/all_gather | solution.py:45
  1156.4 11.5 multiply_reduce_fusion
  1167.9 0.0 all-gather.9.cloned.1.call-update
  1167.9 5.9 copy.13
  1173.8 98.7 %all-gather.9.cloned.1.call-done = f32[262144]{0:T(1024)} async-done(((f32[2048]{0:T(1024)}), f32[262144]{0:T(1024)}) %all-gather.9.cloned.1.call-update) | async-done | bytes 1048592 | tf_op jit(solution)/shard_map/all_gather | solution.py:51
  1272.5 2.4 reshape.12
  1274.9 1.9 reduce_sum.59
  (10 shorter events, 0.1 us)
Async XLA Ops:
  7.2 95.5 %copy-start = (bf16[2048,640]{1,0:T(8,128)(2,1)S(1)}, bf16[2048,640]{1,0:T(8,128)(2,1)}, u32[]{:S(2)}) copy-start(bf16[2048,640]{1,0:T(8,128)(2,1)} %param.10) | copy-start | bytes 7864324
  7.2 77.4 %all-gather.5.cloned.1.call-start = ((), (), s32[]{:S(2)}) async-start(), calls=%async_computation.2 | async-start | bytes 6127616 | tf_op jit(solution)/shard_map/all_gather | solution.py:14
  15.5 131.2 %reduce-scatter.5.cloned.1.call-start = ((), (), s32[]{:S(2)}) async-start(), calls=%async_computation.4 | async-start | bytes 5406720 | tf_op jit(solution)/shard_map/reduce_scatter | solution.py:23
  94.5 0.7 copy-start.2
  94.5 8.1 copy-start.3
  94.6 385.4 %reduce-scatter.3.cloned.1.call-start = ((), (), s32[]{:S(2)}) async-start(), calls=%async_computation.3 | async-start | bytes 5406720 | tf_op jit(solution)/shard_map/reduce_scatter | solution.py:24
  111.9 0.7 copy-start.1
  111.9 1044.5 %all-gather.7.cloned.1.call-start = ((), (), s32[]{:S(2)}) async-start(), calls=%async_computation.5 | async-start | bytes 2703360 | tf_op jit(solution)/shard_map/all_gather | solution.py:45
  1130.4 142.1 %all-gather.9.cloned.1.call-start = ((), (), s32[]{:S(2)}) async-start(), calls=%async_computation.6 | async-start | bytes 1056768 | tf_op jit(solution)/shard_map/all_gather | solution.py:51
Sparse Core Ops, SparseCore 0:
  15.6 68.9 all-gather.4
  94.7 51.9 reduce-scatter.4
  149.3 54.8 reduce-scatter.2
  1130.5 25.8 all-gather.6
  1168.0 104.4 all-gather.8
